TPU v7x, 32 devices: a whole 2x2x4 slice. The times are simulated.
32 devices in a mesh: dp: 8 (over z, x), tensor: 4 (over y, core).
Axes of the slice: x: 2, y: 2, z: 4, core: 2. Of those that a mesh axis runs over, the one named last changes fastest.
Arguments:
- hidden: float32 [8192, 640], P('dp'), may hold values from -6 to 6
- seq_lengths: int32 [8, 4], P('dp'), may hold values from 0 to 1024, as said below
- input_scale: float32 [640], replicated, may hold values from 0.25 to 1.75
- w_query: float32 [640, 1024], P(None, 'tensor'), may hold values from -0.25 to 0.25
- w_key: float32 [640, 256], replicated, may hold values from -0.25 to 0.25
- w_value: float32 [640, 256], replicated, may hold values from -0.25 to 0.25
- query_scale: float32 [256], replicated, may hold values from 0.25 to 1.75
- key_scale: float32 [256], replicated, may hold values from 0.25 to 1.75
- w_out: float32 [1024, 640], P('tensor'), may hold values from -0.1875 to 0.1875
- post_attn_scale: float32 [640], replicated, may hold values from 0.25 to 1.75
- pre_ffn_scale: float32 [640], replicated, may hold values from 0.25 to 1.75
- w_gate: float32 [640, 2048], P(None, 'tensor'), may hold values from -0.25 to 0.25
- w_up: float32 [640, 2048], P(None, 'tensor'), may hold values from -0.25 to 0.25
- w_down: float32 [2048, 640], P('tensor'), may hold values from -0.125 to 0.125
- post_ffn_scale: float32 [640], replicated, may hold values from 0.25 to 1.75
- out_cotangent: float32 [8192, 640], P('dp'), may hold values from -6 to 6
Outputs:
- output: float32 [8192, 640], P('dp')
- hidden_grad: float32 [8192, 640], P('dp')
- input_scale_grad: float32 [640], replicated
- w_query_grad: float32 [640, 1024], P(None, 'tensor')
- w_key_grad: float32 [640, 256], replicated
- w_value_grad: float32 [640, 256], replicated
- query_scale_grad: float32 [256], replicated
- key_scale_grad: float32 [256], replicated
- w_out_grad: float32 [1024, 640], P('tensor')
- post_attn_scale_grad: float32 [640], replicated
- pre_ffn_scale_grad: float32 [640], replicated
- w_gate_grad: float32 [640, 2048], P(None, 'tensor')
- w_up_grad: float32 [640, 2048], P(None, 'tensor')
- w_down_grad: float32 [2048, 640], P('tensor')
- post_ffn_scale_grad: float32 [640], replicated
Inputs may be any that keep to these rules, and one draw needn't show every extreme that they name: `seq_lengths`: row d lists the lengths of the sequences held by index d of dp, in slot order, zeros for unused sequence slots; a row sums to at most 1024. In every draw exactly one row is a single sequence of 1024 tokens followed by zeros; every other row sums to between 128 and 896.
All inputs are finite; a program needn't handle non-finite values.
Results may differ from a plain program's by a relative error of at most 0.0003.
Values sent between devices are 32-bit elements; how exact they have to be, the bound alone decides.
A program may use at most 128 MiB of HBM per device.

v0:
```python
from functools import partial
import jax
import jax.numpy as jnp
from jax import lax
from jax.sharding import PartitionSpec as P

WINDOW = 512
epsilon = 1e-06
highest = lax.Precision.HIGHEST


def root_scale(values, gain):
    return values * lax.rsqrt(jnp.mean(values * values, axis=-1, keepdims=True) + epsilon) * gain


def rotate(values, cosine, sine):
    half_dim = values.shape[-1] // 2
    first_half = values[..., :half_dim]
    second_half = values[..., half_dim:]
    return jnp.concatenate(
        [first_half * cosine - second_half * sine, second_half * cosine + first_half * sine],
        axis=-1,
    )


def layout(lengths, row_count):
    bounds = jnp.concatenate([jnp.zeros((1,), jnp.int32), jnp.cumsum(lengths)])
    slot_index = jnp.arange(row_count, dtype=jnp.int32)
    segment = jnp.sum((slot_index[:, None] >= bounds[None, 1:]).astype(jnp.int32), axis=1)
    starts = jnp.max(jnp.where(bounds[None, :] <= slot_index[:, None], bounds[None, :], 0), axis=1)
    return (segment, slot_index - starts, slot_index < bounds[-1], slot_index)


def tables(positions, head_dim):
    half_dim = head_dim // 2
    frequency = 10000.0 ** (-2.0 * jnp.arange(half_dim).astype(jnp.float32) / head_dim)
    angles = positions.astype(jnp.float32)[:, None] * frequency[None, :]
    return (jnp.cos(angles), jnp.sin(angles))


def project_rows(inputs, gain, query_w, key_w, value_w, query_gain, key_gain, cosine, sine):
    normed = root_scale(inputs, gain)
    row_count = inputs.shape[0]
    queries = jnp.dot(normed, query_w, precision=highest).reshape(row_count, -1, key_w.shape[1])
    key_rows = jnp.dot(normed, key_w, precision=highest)
    value_rows = jnp.dot(normed, value_w, precision=highest)
    queries = rotate(root_scale(queries, query_gain), cosine[:, None, :], sine[:, None, :])
    key_rows = rotate(root_scale(key_rows, key_gain), cosine, sine)
    return (queries, key_rows, value_rows)


def middle(residual, branch, branch_gain, next_gain):
    hid_rows = residual + root_scale(branch, branch_gain)
    return (hid_rows, root_scale(hid_rows, next_gain))


def feed(inputs, gate_w, up_w, down_w):
    gated = jax.nn.gelu(jnp.dot(inputs, gate_w, precision=highest), approximate=True) * jnp.dot(
        inputs, up_w, precision=highest
    )
    return jnp.dot(gated, down_w, precision=highest)


def finish(branch, gain, residual):
    return residual + root_scale(branch, gain)


def on_device(
    hidden,
    seq_lengths,
    input_scale,
    w_query,
    w_key,
    w_value,
    query_scale,
    key_scale,
    w_out,
    post_attn_scale,
    pre_ffn_scale,
    w_gate,
    w_up,
    w_down,
    post_ffn_scale,
    out_cotangent,
):
    row_count = hidden.shape[0]
    head_dim = w_key.shape[1]
    head_count = w_query.shape[1] // head_dim
    scale = head_dim ** (-0.5)
    segment, positions, live_mask, slot_index = layout(seq_lengths[0], row_count)
    cosine, sine = tables(positions, head_dim)
    live_rows = live_mask.astype(jnp.float32)[:, None]
    (queries, key_rows, value_rows), project_back = jax.vjp(
        partial(project_rows, cosine=cosine, sine=sine),
        hidden,
        input_scale,
        w_query,
        w_key,
        w_value,
        query_scale,
        key_scale,
    )
    block_rows = min(512, row_count)
    block_count = row_count // block_rows
    key_pad = jnp.concatenate([jnp.zeros((block_rows, head_dim), jnp.float32), key_rows], axis=0)
    value_pad = jnp.concatenate(
        [jnp.zeros((block_rows, head_dim), jnp.float32), value_rows], axis=0
    )
    segment_pad = jnp.concatenate([jnp.full((block_rows,), -1, jnp.int32), segment])
    slot_pad = jnp.concatenate([jnp.arange(-block_rows, 0, dtype=jnp.int32), slot_index])

    def block_inputs(block_index):
        first_row = block_index * block_rows
        query_block = lax.dynamic_slice_in_dim(queries, first_row, block_rows, 0)
        key_block = lax.dynamic_slice_in_dim(key_pad, first_row, 2 * block_rows, 0)
        value_block = lax.dynamic_slice_in_dim(value_pad, first_row, 2 * block_rows, 0)
        distance = (
            lax.dynamic_slice_in_dim(slot_index, first_row, block_rows, 0)[:, None]
            - lax.dynamic_slice_in_dim(slot_pad, first_row, 2 * block_rows, 0)[None, :]
        )
        same_segment = (
            lax.dynamic_slice_in_dim(segment, first_row, block_rows, 0)[:, None]
            == lax.dynamic_slice_in_dim(segment_pad, first_row, 2 * block_rows, 0)[None, :]
        )
        allowed = same_segment & (distance >= 0) & (distance < WINDOW)
        scores = jnp.einsum("ihd,jd->hij", query_block, key_block, precision=highest) * scale
        scores = jnp.where(allowed[None], scores, -1e30)
        return (query_block, key_block, value_block, allowed, scores)

    def attend_block(block_index):
        query_block, key_block, value_block, allowed, scores = block_inputs(block_index)
        row_max = jnp.max(scores, axis=-1, keepdims=True)
        weights = jnp.exp(scores - row_max)
        weight_sum = jnp.sum(weights, axis=-1, keepdims=True)
        mixed_block = jnp.einsum(
            "hij,jd->ihd", weights / weight_sum, value_block, precision=highest
        )
        return (mixed_block, (row_max + jnp.log(weight_sum))[..., 0])

    def forward_block(block_index):
        return attend_block(block_index)

    mixed_blocks, log_sums = lax.map(forward_block, jnp.arange(block_count))
    mixed = mixed_blocks.reshape(row_count, head_count * head_dim)
    attn_part = jnp.dot(mixed, w_out, precision=highest)
    attn_whole = lax.psum(attn_part, "tensor")
    (hid_rows, ffn_in), middle_back = jax.vjp(
        middle, hidden, attn_whole, post_attn_scale, pre_ffn_scale
    )
    mlp_part, feed_back = jax.vjp(feed, ffn_in, w_gate, w_up, w_down)
    mlp_whole = lax.psum(mlp_part, "tensor")
    result, finish_back = jax.vjp(finish, mlp_whole, post_ffn_scale, hid_rows)
    output = result * live_rows
    out_grad = out_cotangent * live_rows
    mlp_grad, post_ffn_grad, hid_direct = finish_back(out_grad)
    ffn_in_part, gate_grad, up_grad, down_grad = feed_back(mlp_grad)
    ffn_in_grad = lax.psum(ffn_in_part, "tensor")
    hidden_direct, attn_grad, post_attn_grad, pre_ffn_grad = middle_back((hid_direct, ffn_in_grad))
    mixed_grad = jnp.dot(attn_grad, w_out.T, precision=highest).reshape(
        row_count, head_count, head_dim
    )
    out_weight_grad = jnp.dot(mixed.T, attn_grad, precision=highest)
    row_dots = jnp.sum(mixed_grad * mixed_blocks.reshape(row_count, head_count, head_dim), axis=-1)

    def attend_back(running, block_index):
        key_acc, value_acc = running
        query_block, key_block, value_block, allowed, scores = block_inputs(block_index)
        first_row = block_index * block_rows
        grad_block = lax.dynamic_slice_in_dim(mixed_grad, first_row, block_rows, 0)
        dots_block = lax.dynamic_slice_in_dim(row_dots, first_row, block_rows, 0)
        weights = jnp.where(allowed[None], jnp.exp(scores - log_sums[block_index][:, :, None]), 0.0)
        value_part = jnp.einsum("hij,ihd->jd", weights, grad_block, precision=highest)
        spread = jnp.einsum("ihd,jd->hij", grad_block, value_block, precision=highest)
        score_grad = weights * (spread - dots_block.T[:, :, None])
        query_part = jnp.einsum("hij,jd->ihd", score_grad, key_block, precision=highest) * scale
        key_part = jnp.einsum("hij,ihd->jd", score_grad, query_block, precision=highest) * scale
        key_acc = lax.dynamic_update_slice_in_dim(
            key_acc,
            lax.dynamic_slice_in_dim(key_acc, first_row, 2 * block_rows, 0) + key_part,
            first_row,
            0,
        )
        value_acc = lax.dynamic_update_slice_in_dim(
            value_acc,
            lax.dynamic_slice_in_dim(value_acc, first_row, 2 * block_rows, 0) + value_part,
            first_row,
            0,
        )
        return ((key_acc, value_acc), query_part)

    def back_block(running, block_index):
        return attend_back(running, block_index)

    empty_pad = jnp.zeros((row_count + block_rows, head_dim), jnp.float32)
    (key_acc, value_acc), query_parts = lax.scan(
        back_block, (empty_pad, empty_pad), jnp.arange(block_count)
    )
    query_grad = query_parts.reshape(row_count, head_count, head_dim)
    (
        hidden_part,
        input_part,
        query_w_grad,
        key_w_grad,
        value_w_grad,
        query_gain_grad,
        key_gain_grad,
    ) = project_back((query_grad, key_acc[block_rows:], value_acc[block_rows:]))
    hidden_attn, input_grad = lax.psum((hidden_part, input_part), "tensor")
    hidden_grad = hidden_direct + hidden_attn
    (
        query_w_grad,
        out_weight_grad,
        gate_grad,
        up_grad,
        down_grad,
        input_grad,
        post_attn_grad,
        pre_ffn_grad,
        post_ffn_grad,
    ) = lax.psum(
        (
            query_w_grad,
            out_weight_grad,
            gate_grad,
            up_grad,
            down_grad,
            input_grad,
            post_attn_grad,
            pre_ffn_grad,
            post_ffn_grad,
        ),
        "dp",
    )
    key_w_grad, value_w_grad, query_gain_grad, key_gain_grad = lax.psum(
        (key_w_grad, value_w_grad, query_gain_grad, key_gain_grad), ("dp", "tensor")
    )
    return (
        output,
        hidden_grad,
        input_grad,
        query_w_grad,
        key_w_grad,
        value_w_grad,
        query_gain_grad,
        key_gain_grad,
        out_weight_grad,
        post_attn_grad,
        pre_ffn_grad,
        gate_grad,
        up_grad,
        down_grad,
        post_ffn_grad,
    )


def solution(mesh):
    placed = (
        P("dp", None),
        P("dp", None),
        P(),
        P(None, "tensor"),
        P(),
        P(),
        P(),
        P(),
        P("tensor", None),
        P(),
        P(),
        P(None, "tensor"),
        P(None, "tensor"),
        P("tensor", None),
        P(),
        P("dp", None),
    )
    return jax.shard_map(
        on_device,
        mesh=mesh,
        in_specs=placed,
        out_specs=(
            P("dp", None),
            P("dp", None),
            P(),
            P(None, "tensor"),
            P(),
            P(),
            P(),
            P(),
            P("tensor", None),
            P(),
            P(),
            P(None, "tensor"),
            P(None, "tensor"),
            P("tensor", None),
            P(),
        ),
        check_vma=False,
    )
```

profile of v0, /device:TPU:0, one launch (start us, length us, event | category | flops | bytes accessed | tf_op | source)
XLA Modules:
  0.0 843.5 jit_solution(12557632794079602929)
XLA Ops:
  40.6 44.3 %while.26 = (s32[]{:T(128)}, f32[2,512,1,256]{1,0,3,2:T(2,128)}, f32[2,1,512]{2,1,0:T(1,128)}, s32[2]{0:T(128)S(1)}, f32[1536,256]{1,0:T(8,128)}, /*index=5*/s32...) while((s32[]{:T(128)}, f32[2,512,1,256]{1,0,3,2:T(2,128)}, ...), condition=%wide.region_9.10_spmd, body=%wide.region_6.9_spmd.sunk | while | flops 3228040704 | bytes 18932016 | solution.py:143
  52.4 10.3 %dynamic_update_slice.26 = f32[2,512,1,256]{1,0,3,2:T(2,128)} dynamic-update-slice(f32[2,512,1,256]{1,0,3,2:T(2,128)} %get-tuple-element.486, f32[1,512,1,256]{1,0,3,2:T(1,128)S(1)} %copy.111, s32[]{:T(128)S(6)} %copy.125, s32[]{:T(128)} %constant.60.clone.1..sunk, s32[]{:T(128)} %constant.60.clone.1..sunk, s32[]{:T(128)} %constant.60.clone.1..sunk) | dynamic-update-slice | bytes 1048580 | tf_op jit(solution)/shard_map/while/body/jit(dynamic_update_index_in_dim)/dynamic_update_slice | solution.py:143
  74.5 10.3 %dynamic_update_slice.26 = f32[2,512,1,256]{1,0,3,2:T(2,128)} dynamic-update-slice(f32[2,512,1,256]{1,0,3,2:T(2,128)} %get-tuple-element.486, f32[1,512,1,256]{1,0,3,2:T(1,128)S(1)} %copy.111, s32[]{:T(128)S(6)} %copy.125, s32[]{:T(128)} %constant.60.clone.1..sunk, s32[]{:T(128)} %constant.60.clone.1..sunk, s32[]{:T(128)} %constant.60.clone.1..sunk) | dynamic-update-slice | bytes 1048580 | tf_op jit(solution)/shard_map/while/body/jit(dynamic_update_index_in_dim)/dynamic_update_slice | solution.py:143
  91.9 62.3 %all-reduce.18.cloned.1.call-done = f32[1024,640]{1,0:T(8,128)} async-done(((f32[1024,640]{1,0:T(8,128)}), f32[1024,640]{1,0:T(8,128)}) %all-reduce.18.cloned.1.call-update) | async-done | bytes 2621456 | tf_op jit(solution)/shard_map/psum | solution.py:146
  171.0 7.4 fusion.121
  180.3 58.3 %all-reduce.20.cloned.1.call-done = f32[1024,640]{1,0:T(8,128)} async-done(((f32[1024,640]{1,0:T(8,128)}), f32[1024,640]{1,0:T(8,128)}) %all-reduce.20.cloned.1.call-update) | async-done | bytes 2621456 | tf_op jit(solution)/shard_map/psum | solution.py:151
  251.8 5.8 fusion.124
  257.7 8.5 %convolution_add_fusion = f32[1024,640]{1,0:T(8,128)} fusion(f32[1024,640]{1,0:T(8,128)S(1)} %fusion.124, f32[640,512]{1,0:T(8,128)S(1)} %copy-done.61, f32[1024,512]{1,0:T(8,128)S(1)} %copy-done.29, f32[1024,512]{1,0:T(8,128)S(1)} %fusion.133, f32[1024,512]{1,0:T(8,128)S(1)} %copy-done.44), kind=kOutput, calls=%fused_computation.94 | convolution fusion | flops 4037672960 | bytes 12845056 | tf_op jit(solution)/shard_map/transpose(jvp())/dot_general | solution.py:58
  266.3 9.4 %fusion.67 = f32[640,512]{1,0:T(8,128)} fusion(f32[1024,640]{1,0:T(8,128)} %copy-done.6, f32[640]{0:T(1024)S(1)} %copy-done.77, f32[1024]{0:T(1024)S(1)} %fusion.117, f32[1024,512]{1,0:T(8,128)} %copy-done.46, f32[1024,512]{1,0:T(8,128)} %copy-done.28), kind=kOutput, calls=%fused_computation.95 | convolution fusion | flops 4032561152 | bytes 8133120 | tf_op jit(solution)/shard_map/transpose(jvp())/dot_general | solution.py:58
  275.8 7.2 fusion.68
  283.0 43.4 %all-reduce.22.cloned.1.call-done = f32[1024,640]{1,0:T(8,128)} async-done(((f32[1024,640]{1,0:T(8,128)}), f32[1024,640]{1,0:T(8,128)}) %all-reduce.22.cloned.1.call-update) | async-done | bytes 2621456 | tf_op jit(solution)/shard_map/psum | solution.py:157
  342.3 68.0 %while.27 = (s32[]{:T(128)}, f32[1536,256]{0,1:T(8,128)}, f32[1536,256]{1,0:T(8,128)}, f32[2,512,1,256]{1,0,3,2:T(2,128)}, s32[2]{0:T(128)S(1)}, /*index=5*/s32[...) while((s32[]{:T(128)}, f32[1536,256]{0,1:T(8,128)}, ...), condition=%wide.region_21.22_spmd, body=%wide.region_20.21_spmd.sunk | while | flops 8060272640 | bytes 59294212 | solution.py:195
  366.0 10.3 %dynamic_update_slice.29 = f32[2,512,1,256]{1,0,3,2:T(2,128)} dynamic-update-slice(f32[2,512,1,256]{1,0,3,2:T(2,128)} %get-tuple-element.541, f32[1,512,1,256]{1,0,3,2:T(1,128)S(1)} %copy.116, s32[]{:T(128)S(6)} %copy.138, s32[]{:T(128)} %constant.60.clone.1..sunk.1, s32[]{:T(128)} %constant.60.clone.1..sunk.1, s32[]{:T(128)} %constant.60.clone.1..sunk.1) | dynamic-update-slice | bytes 1048580 | tf_op jit(solution)/shard_map/while/body/jit(dynamic_update_index_in_dim)/dynamic_update_slice | solution.py:143
  399.9 10.3 %dynamic_update_slice.29 = f32[2,512,1,256]{1,0,3,2:T(2,128)} dynamic-update-slice(f32[2,512,1,256]{1,0,3,2:T(2,128)} %get-tuple-element.541, f32[1,512,1,256]{1,0,3,2:T(1,128)S(1)} %copy.116, s32[]{:T(128)S(6)} %copy.138, s32[]{:T(128)} %constant.60.clone.1..sunk.1, s32[]{:T(128)} %constant.60.clone.1..sunk.1, s32[]{:T(128)} %constant.60.clone.1..sunk.1) | dynamic-update-slice | bytes 1048580 | tf_op jit(solution)/shard_map/while/body/jit(dynamic_update_index_in_dim)/dynamic_update_slice | solution.py:143
  430.7 6.1 multiply_reduce_fusion.3
  440.6 10.8 %fusion.119 = f32[512,640]{1,0:T(8,128)} fusion(f32[1024,512]{1,0:T(8,128)} %copy-done.43, f32[1024,512]{1,0:T(8,128)S(1)} %copy-done.31, f32[1024,640]{1,0:T(8,128)} %all-reduce.20.cloned.1.call-done, f32[1024,640]{1,0:T(8,128)} %param.35, f32[1024]{0:T(1024)S(1)} %copy-done.93, f32[1024]{0:T(1024)S(1)} %copy-done.76, f32[640]{0:T(1024)S(1)} %copy-done.91, ...), kind=kOutput, calls=%fused_computation.188 | convolution fusion | flops 4035182592 | bytes 10762752 | tf_op jit(solution)/shard_map/transpose(jvp())/dot_general | solution.py:61
  451.4 6.6 fusion.82
  458.1 5.6 fusion.129
  463.9 7.3 fusion.126
  475.3 39.7 %all-reduce.7 = (f32[256]{0:T(256)}, f32[256]{0:T(256)}) all-reduce(f32[256]{0:T(256)S(1)} %get-tuple-element.219, f32[256]{0:T(256)S(1)} %get-tuple-element.217), channel_id=1, replica_groups=mesh['dp'=8,'tensor'=4] {'dp','tensor'}, use_global_device_ids=true, to_apply=%region_33.34 | all-reduce | flops 512 | bytes 4096 | tf_op jit(solution)/shard_map/psum | solution.py:234
  515.0 7.1 psum.130
  522.0 36.2 %all-reduce.9 = (f32[640]{0:T(1024)}, f32[640]{0:T(1024)}, f32[640]{0:T(1024)}, f32[640]{0:T(1024)}) all-reduce(f32[640]{0:T(1024)S(1)} %psum.130, f32[640]{0:T(1024)S(1)} %get-tuple-element.213, f32[640]{0:T(1024)S(1)} %get-tuple-element.211, f32[640]{0:T(1024)S(1)} %copy-done.94), channel_id=1, replica_groups=mesh['dp'=8,'tensor'=4] {'dp'}, use_global_device_ids=true, to_apply=%region_28.29 | all-reduce | flops 2560 | bytes 20480 | tf_op jit(solution)/shard_map/psum | solution.py:220
  562.5 75.1 %all-reduce.26.cloned.1.call-done = (f32[640,256]{1,0:T(8,128)}, f32[640,256]{1,0:T(8,128)}) async-done(((f32[640,256]{1,0:T(8,128)}, f32[640,256]{1,0:T(8,128)}), (f32[640,256]{1,0:T(8,128)}, f32[640,256]{1,0:T(8,128)})) %all-reduce.26.cloned.1.call-update) | async-done | bytes 1310736 | tf_op jit(solution)/shard_map/psum | solution.py:234
  637.6 189.8 %all-reduce.28.cloned.1.call-done = (f32[640,256]{1,0:T(8,128)}, f32[256,640]{1,0:T(8,128)}, f32[640,512]{1,0:T(8,128)}, f32[640,512]{1,0:T(8,128)}, f32[512,640]{1,0:T(8,128)}) async-done(((f32[640,256]{1,0:T(8,128)}, f32[256,640]{1,0:T(8,128)}, f32[640,512]{1,0:T(8,128)}, f32[640,512]{1,0:T(8,128)}, f32[512,640]{1,0:T(8,128)}), (f32[640,256]{1,0:T(8,128)}, f32[256,640]{1,0:T(8,128)}, ...) | async-done | bytes 5242896 | tf_op jit(solution)/shard_map/psum | solution.py:220
  (359 shorter events, 193.2 us)
Async XLA Ops:
  7.2 163.9 %copy-start = (f32[512,640]{1,0:T(8,128)S(1)}, f32[512,640]{1,0:T(8,128)}, u32[]{:S(2)}) copy-start(f32[512,640]{1,0:T(8,128)} %param.33) | copy-start | bytes 3932164
  7.2 147.0 %all-reduce.18.cloned.1.call-start = ((), (), s32[]{:S(2)}) async-start(), calls=%async_computation | async-start | bytes 5242880 | tf_op jit(solution)/shard_map/psum | solution.py:146
  7.3 21.2 %copy-start.95 = (f32[128]{0:T(128)}, f32[128]{0:T(128)S(1)}, u32[]{:S(2)}) copy-start(f32[128]{0:T(128)S(1)} %multiply_power_fusion) | copy-start | bytes 1540
  9.1 19.4 %copy-start.67 = (f32[1024]{0:T(1024)}, f32[1024]{0:T(1024)S(1)}, u32[]{:S(2)}) copy-start(f32[1024]{0:T(1024)S(1)} %subtract_convert_fusion) | copy-start | bytes 12292
  91.5 64.9 %copy-start.73 = (f32[640]{0:T(1024)S(1)}, f32[640]{0:T(1024)}, u32[]{:S(2)}) copy-start(f32[640]{0:T(1024)} %param.29) | copy-start | bytes 7684
  91.5 147.1 %all-reduce.20.cloned.1.call-start = ((), (), s32[]{:S(2)}) async-start(), calls=%async_computation.1 | async-start | bytes 5242880 | tf_op jit(solution)/shard_map/psum | solution.py:151
  156.8 177.4 %copy-start.65 = (f32[1024]{0:T(1024)}, f32[1024]{0:T(1024)S(1)}, u32[]{:S(2)}) copy-start(f32[1024]{0:T(1024)S(1)} %fusion.116) | copy-start | bytes 12292
  178.4 62.3 %copy-start.90 = (f32[640]{0:T(1024)S(1)}, f32[640]{0:T(1024)}, u32[]{:S(2)}) copy-start(f32[640]{0:T(1024)} %param.34) | copy-start | bytes 7684
  178.4 148.0 %all-reduce.22.cloned.1.call-start = ((), (), s32[]{:S(2)}) async-start(), calls=%async_computation.2 | async-start | bytes 5242880 | tf_op jit(solution)/shard_map/psum | solution.py:157
  180.3 149.7 %copy-start.75 = (f32[1024]{0:T(1024)}, f32[1024]{0:T(1024)S(1)}, u32[]{:S(2)}) copy-start(f32[1024]{0:T(1024)S(1)} %fusion.112) | copy-start | bytes 12292
  266.3 292.0 %all-reduce.24.cloned.1.call-start = ((), (), s32[]{:S(2)}) async-start(), calls=%async_computation.3 | async-start | bytes 5242880 | tf_op jit(solution)/shard_map/psum | solution.py:208
  266.3 9.4 %copy-start.8 = (f32[1024,640]{1,0:T(8,128)S(1)}, f32[1024,640]{1,0:T(8,128)}, u32[]{:S(2)}) copy-start(f32[1024,640]{1,0:T(8,128)} %copy-done.6) | copy-start | bytes 7864324
  266.3 9.4 %copy-start.30 = (f32[1024,512]{1,0:T(8,128)S(1)}, f32[1024,512]{1,0:T(8,128)}, u32[]{:S(2)}) copy-start(f32[1024,512]{1,0:T(8,128)} %copy-done.28) | copy-start | bytes 6291460
  266.3 9.4 %copy-start.45 = (f32[1024,512]{1,0:T(8,128)S(1)}, f32[1024,512]{1,0:T(8,128)}, u32[]{:S(2)}) copy-start(f32[1024,512]{1,0:T(8,128)} %copy-done.43) | copy-start | bytes 6291460
  266.3 9.4 %copy-start.47 = (f32[1024,512]{1,0:T(8,128)S(1)}, f32[1024,512]{1,0:T(8,128)}, u32[]{:S(2)}) copy-start(f32[1024,512]{1,0:T(8,128)} %copy-done.46) | copy-start | bytes 6291460
  364.9 11.5 %copy-start.17 = (f32[1024,1,256]{2,1,0:T(1,128)S(1)}, f32[1024,1,256]{2,1,0:T(1,128)}, u32[]{:S(2)}) copy-start(f32[1024,1,256]{2,1,0:T(1,128)} %copy-done.16) | copy-start | bytes 3145732 | tf_op jit(solution)/shard_map/while
  398.8 11.5 %copy-start.17 = (f32[1024,1,256]{2,1,0:T(1,128)S(1)}, f32[1024,1,256]{2,1,0:T(1,128)}, u32[]{:S(2)}) copy-start(f32[1024,1,256]{2,1,0:T(1,128)} %copy-done.16) | copy-start | bytes 3145732 | tf_op jit(solution)/shard_map/while
  417.3 13.4 %copy-start.35 = (f32[1024,1,128]{0,2,1:T(8,128)}, f32[1024,1,128]{0,2,1:T(8,128)S(1)}, u32[]{:S(2)}) copy-start(f32[1024,1,128]{0,2,1:T(8,128)S(1)} %get-tuple-element.294) | copy-start | bytes 1572868
  417.3 13.4 %copy-start.37 = (f32[1024,1,128]{0,2,1:T(8,128)}, f32[1024,1,128]{0,2,1:T(8,128)S(1)}, u32[]{:S(2)}) copy-start(f32[1024,1,128]{0,2,1:T(8,128)S(1)} %get-tuple-element.295) | copy-start | bytes 1572868
  439.0 198.6 %all-reduce.26.cloned.1.call-start = ((), (), s32[]{:S(2)}) async-start(), calls=%async_computation.4 | async-start | bytes 2621440 | tf_op jit(solution)/shard_map/psum | solution.py:234
  440.6 10.8 %copy-start.5 = (f32[1024,640]{1,0:T(8,128)S(1)}, f32[1024,640]{1,0:T(8,128)}, u32[]{:S(2)}) copy-start(f32[1024,640]{1,0:T(8,128)} %param.20) | copy-start | bytes 7864324
  463.8 363.7 %all-reduce.28.cloned.1.call-start = ((), (), s32[]{:S(2)}) async-start(), calls=%async_computation.5 | async-start | bytes 10485760 | tf_op jit(solution)/shard_map/psum | solution.py:220
  475.2 46.8 %copy-start.94 = (f32[640]{0:T(1024)S(1)}, f32[640]{0:T(1024)}, u32[]{:S(2)}) copy-start(f32[640]{0:T(1024)} %get-tuple-element.209) | copy-start | bytes 7684
  637.6 193.9 %copy-start.62 = (f32[640,256]{1,0:T(8,128)S(1)}, f32[640,256]{1,0:T(8,128)}, u32[]{:S(2)}) copy-start(f32[640,256]{1,0:T(8,128)} %get-tuple-element.585) | copy-start | bytes 1966084
  (87 other events, 343.3 us)
Sparse Core Ops, SparseCore 0:
  91.6 62.5 all-reduce.17
  178.5 59.9 all-reduce.19
  266.4 59.9 all-reduce.21
  439.1 60.6 all-reduce.23
  505.9 131.7 all-reduce.25
  643.0 184.4 all-reduce.27
where the time goes:
time: 852 us; the launch traced here: 844 us
  waiting for transfers between devices  429 us (50%)
  matrix products  165 us (19%)
  local copies, waits for them, and re-layouts  100 us (12%)
  blocking collectives  82.9 us (10%)
  other arithmetic  43.3 us (5%)
  between operations  15.5 us (2%)
    psum x1, waiting for transfers between devices, on_device(): lax.psum((query_w_grad, out_weight_grad, gate_grad, up_grad, down_grad, i...  190 us
    psum x1, waiting for transfers between devices, on_device(): lax.psum((key_w_grad, value_w_grad, query_gain_grad, key_gain_grad), ('dp...  75.1 us
    psum x1, waiting for transfers between devices, on_device(): attn_whole = lax.psum(attn_part, 'tensor')  62.3 us
    psum x1, waiting for transfers between devices, on_device(): mlp_whole = lax.psum(mlp_part, 'tensor')  58.3 us
    dynamic_update_slice x10, local copies, waits for them, and re-layouts, on_device(): mixed_blocks, log_sums = lax.map(forward_block, jnp.arange(block_count))  44.6 us
    psum x1, waiting for transfers between devices, on_device(): ffn_in_grad = lax.psum(ffn_in_part, 'tensor')  43.4 us
    psum x1, blocking collectives, on_device(): lax.psum((key_w_grad, value_w_grad, query_gain_grad, key_gain_grad), ('dp...  39.7 us
    psum x1, blocking collectives, on_device(): lax.psum((query_w_grad, out_weight_grad, gate_grad, up_grad, down_grad, i...  36.2 us
  transfers between devices with their start and end apart: 6, of which 5 were waited for; matrix products, arithmetic and copies ran while one was open for 7% of the time, Pallas kernels for 0%

commit v1 on v0

--- a/solution.py
+++ b/solution.py
@@ -231,8 +231,16 @@
         ),
         "dp",
     )
-    key_w_grad, value_w_grad, query_gain_grad, key_gain_grad = lax.psum(
-        (key_w_grad, value_w_grad, query_gain_grad, key_gain_grad), ("dp", "tensor")
+
+    def test_vector(chunk):
+        row_axis = "dp"
+        lane_axis = "tensor"
+        for src_i in (lane_axis, row_axis):
+            chunk = lax.psum(chunk, src_i)
+        return chunk
+
+    key_w_grad, value_w_grad, query_gain_grad, key_gain_grad = test_vector(
+        (key_w_grad, value_w_grad, query_gain_grad, key_gain_grad)
     )
     return (
         output,

time: 852 us -> 777 us (0.912)
  blocking collectives: 82.9 us -> 45.8 us
  local copies, waits for them, and re-layouts: 100 us -> 75.7 us
  waiting for transfers between devices: 429 us -> 407 us
  matrix products: 165 us -> 179 us
    psum x1 -> x0, waiting for transfers between devices: 75.1 us -> none  [on_device(): lax.psum((key_w_grad, value_w_grad, query_gain_grad, key_gain_grad), ('dp...]
    psum x1, waiting for transfers between devices: 0.01 us -> 54.5 us  [on_device(): hidden_attn, input_grad = lax.psum((hidden_part, input_part), 'tensor')]
    psum x1 -> x0, blocking collectives: 39.7 us -> none  [on_device(): lax.psum((key_w_grad, value_w_grad, query_gain_grad, key_gain_grad), ('dp...]
    dynamic_update_slice x10, local copies, waits for them, and re-layouts: 44.6 us -> 32.3 us  [on_device(): mixed_blocks, log_sums = lax.map(forward_block, jnp.arange(block_count))]
    psum x1, waiting for transfers between devices: 190 us -> 181 us  [on_device(): lax.psum((query_w_grad, out_weight_grad, gate_grad, up_grad, down_grad, i...]
    unnamed x195 -> x127, local copies, waits for them, and re-layouts: 18.7 us -> 15.7 us
  transfers between devices with their start and end apart: 6 -> 5, of which waited for: 5 -> 5; matrix products, arithmetic and copies ran while one was open for 7% -> 5% of each run, Pallas kernels for 0% -> 0%
where the time goes in v1:
time: 777 us; the launch traced here: 771 us
  waiting for transfers between devices  407 us (52%)
  matrix products  179 us (23%)
  local copies, waits for them, and re-layouts  75.7 us (10%)
  blocking collectives  45.8 us (6%)
  other arithmetic  40.9 us (5%)
  between operations  14.8 us (2%)
    psum x1, waiting for transfers between devices, on_device(): lax.psum((query_w_grad, out_weight_grad, gate_grad, up_grad, down_grad, i...  181 us
    psum x1, waiting for transfers between devices, on_device(): attn_whole = lax.psum(attn_part, 'tensor')  62.5 us
    psum x1, waiting for transfers between devices, on_device(): mlp_whole = lax.psum(mlp_part, 'tensor')  58.9 us
    psum x1, waiting for transfers between devices, on_device(): hidden_attn, input_grad = lax.psum((hidden_part, input_part), 'tensor')  54.5 us
    psum x1, waiting for transfers between devices, on_device(): ffn_in_grad = lax.psum(ffn_in_part, 'tensor')  49.4 us
    psum x1, blocking collectives, on_device(): lax.psum((query_w_grad, out_weight_grad, gate_grad, up_grad, down_grad, i...  39.9 us
    dynamic_update_slice x10, local copies, waits for them, and re-layouts, on_device(): mixed_blocks, log_sums = lax.map(forward_block, jnp.arange(block_count))  32.3 us
    dot_general x3, matrix products, feed(): return jnp.dot(gated, down_w, precision=highest)  23.9 us
  transfers between devices with their start and end apart: 5, of which 5 were waited for; matrix products, arithmetic and copies ran while one was open for 5% of the time, Pallas kernels for 0%

profile of v1, /device:TPU:0, one launch (start us, length us, event | category | flops | bytes accessed | tf_op | source)
XLA Modules:
  0.0 771.0 jit_solution(17321406752113947427)
XLA Ops:
  34.7 31.6 %while.26 = (s32[]{:T(128)}, f32[2,512,1,256]{1,0,3,2:T(2,128)S(1)}, f32[2,1,512]{2,1,0:T(1,128)S(1)}, s32[2]{0:T(128)S(1)}, f32[1536,256]{1,0:T(8,128)}, /*inde...) while((s32[]{:T(128)}, ...), condition=%wide.region_9.10_spmd, body=%wide.region_6.9_spmd.sunk | while | flops 3228040704 | bytes 12640524 | solution.py:143
  72.0 62.5 %all-reduce.17.cloned.1.call-done = f32[1024,640]{1,0:T(8,128)} async-done(((f32[1024,640]{1,0:T(8,128)}), f32[1024,640]{1,0:T(8,128)}) %all-reduce.17.cloned.1.call-update) | async-done | bytes 2621456 | tf_op jit(solution)/shard_map/psum | solution.py:146
  144.7 5.1 fusion.69
  151.2 7.6 fusion.121
  160.2 58.9 %all-reduce.19.cloned.1.call-done = f32[1024,640]{1,0:T(8,128)} async-done(((f32[1024,640]{1,0:T(8,128)}), f32[1024,640]{1,0:T(8,128)}) %all-reduce.19.cloned.1.call-update) | async-done | bytes 2621456 | tf_op jit(solution)/shard_map/psum | solution.py:151
  226.6 5.6 fusion.133
  232.3 5.8 fusion.124
  238.2 8.3 %convolution_add_fusion = f32[1024,640]{1,0:T(8,128)} fusion(f32[1024,640]{1,0:T(8,128)S(1)} %fusion.124, f32[640,512]{1,0:T(8,128)S(1)} %copy-done.54, f32[1024,512]{1,0:T(8,128)S(1)} %fusion.70, f32[1024,512]{1,0:T(8,128)S(1)} %fusion.133, f32[1024,512]{1,0:T(8,128)S(1)} %copy-done.37), kind=kOutput, calls=%fused_computation.94 | convolution fusion | flops 4037672960 | bytes 12845056 | tf_op jit(solution)/shard_map/transpose(jvp())/dot_general | solution.py:58
  246.5 10.7 %fusion.119 = f32[512,640]{1,0:T(8,128)} fusion(f32[1024,512]{1,0:T(8,128)} %copy-done.36, f32[1024,512]{1,0:T(8,128)S(1)} %fusion.70, f32[1024,640]{1,0:T(8,128)} %all-reduce.19.cloned.1.call-done, f32[1024,640]{1,0:T(8,128)} %param.35, f32[1024]{0:T(1024)S(1)} %multiply_multiply_fusion.15, f32[1024]{0:T(1024)S(1)} %fusion.112, f32[640]{0:T(1024)S(1)} %copy-done.62, ...), kind=kOutput, calls=%fused_computation.188 | convolution fusion | flops 4035182592 | bytes 10762752 | tf_op jit(solution)/shard_map/transpose(jvp())/dot_general | solution.py:61
  257.2 49.4 %all-reduce.21.cloned.1.call-done = f32[1024,640]{1,0:T(8,128)} async-done(((f32[1024,640]{1,0:T(8,128)}), f32[1024,640]{1,0:T(8,128)}) %all-reduce.21.cloned.1.call-update) | async-done | bytes 2621456 | tf_op jit(solution)/shard_map/psum | solution.py:157
  322.7 79.5 %while.27 = (s32[]{:T(128)}, f32[1536,256]{0,1:T(8,128)}, f32[1536,256]{1,0:T(8,128)}, f32[2,512,1,256]{1,0,3,2:T(2,128)}, s32[2]{0:T(128)S(1)}, /*index=5*/s32[...) while((s32[]{:T(128)}, f32[1536,256]{0,1:T(8,128)}, ...), condition=%wide.region_21.22_spmd, body=%wide.region_20.21_spmd.sunk | while | flops 8060272640 | bytes 63488508 | solution.py:195
  348.2 10.3 %dynamic_update_slice.29 = f32[2,512,1,256]{1,0,3,2:T(2,128)} dynamic-update-slice(f32[2,512,1,256]{1,0,3,2:T(2,128)} %get-tuple-element.547, f32[1,512,1,256]{1,0,3,2:T(1,128)S(1)} %copy.116, s32[]{:T(128)} %get-tuple-element.544, s32[]{:T(128)} %constant.60.clone.1..sunk.1, s32[]{:T(128)} %constant.60.clone.1..sunk.1, s32[]{:T(128)} %constant.60.clone.1..sunk.1) | dynamic-update-slice | bytes 1048580 | tf_op jit(solution)/shard_map/while/body/jit(dynamic_update_index_in_dim)/dynamic_update_slice | solution.py:143
  387.7 10.3 %dynamic_update_slice.29 = f32[2,512,1,256]{1,0,3,2:T(2,128)} dynamic-update-slice(f32[2,512,1,256]{1,0,3,2:T(2,128)} %get-tuple-element.547, f32[1,512,1,256]{1,0,3,2:T(1,128)S(1)} %copy.116, s32[]{:T(128)} %get-tuple-element.544, s32[]{:T(128)} %constant.60.clone.1..sunk.1, s32[]{:T(128)} %constant.60.clone.1..sunk.1, s32[]{:T(128)} %constant.60.clone.1..sunk.1) | dynamic-update-slice | bytes 1048580 | tf_op jit(solution)/shard_map/while/body/jit(dynamic_update_index_in_dim)/dynamic_update_slice | solution.py:143
  406.7 5.4 fusion.129
  412.1 6.7 fusion.130
  423.2 5.3 fusion.82
  432.0 7.7 multiply_reduce_fusion.3
  443.3 8.8 %fusion.67 = f32[640,512]{1,0:T(8,128)} fusion(f32[1024,640]{1,0:T(8,128)} %copy-done.9, f32[640]{0:T(1024)S(1)} %copy-done.59, f32[1024]{0:T(1024)S(1)} %fusion.117, f32[1024,512]{1,0:T(8,128)} %copy-done.39, f32[1024,512]{1,0:T(8,128)S(1)} %copy-done.28), kind=kOutput, calls=%fused_computation.95 | convolution fusion | flops 4032561152 | bytes 8133120 | tf_op jit(solution)/shard_map/transpose(jvp())/dot_general | solution.py:58
  452.2 7.2 fusion.68
  459.4 5.6 fusion.126
  469.1 54.5 %all-reduce.25.cloned.1.call-done = (f32[1024,640]{1,0:T(8,128)}, f32[640,256]{1,0:T(8,128)}, f32[640,256]{1,0:T(8,128)}) async-done(((f32[1024,640]{1,0:T(8,128)}, f32[640,256]{1,0:T(8,128)}, f32[640,256]{1,0:T(8,128)}), (f32[1024,640]{1,0:T(8,128)}, f32[640,256]{1,0:T(8,128)}, f32[640,256]{1,0:T(8,128)})) %all-reduce.25.cloned.1.call-update) | async-done | bytes 3932176 | tf_op jit(solution)/shard_map/psum | solution.py:208
  523.6 5.9 all-reduce.9
  529.5 39.9 %all-reduce.7 = (f32[640]{0:T(1024)}, f32[256]{0:T(256)}, f32[256]{0:T(256)}, f32[640]{0:T(1024)}, f32[640]{0:T(1024)}, /*index=5*/f32[640]{0:T(1024)}) all-reduce(f32[640]{0:T(1024)S(1)} %get-tuple-element.286, f32[256]{0:T(256)S(1)} %get-tuple-element.287, ...), channel_id=1, replica_groups=mesh['dp'=8,'tensor'=4] {'dp'}, use_global_device_ids=true, to_apply=%region_28.29 | all-reduce | flops 3072 | bytes 24576 | tf_op jit(solution)/shard_map/psum | solution.py:220
  574.0 181.3 %all-reduce.23.cloned.1.call-done = (f32[640,256]{1,0:T(8,128)}, f32[640,256]{1,0:T(8,128)}, f32[640,256]{1,0:T(8,128)}, f32[256,640]{1,0:T(8,128)}, f32[640,512...) async-done(((f32[640,256]{1,0:T(8,128)}, f32[640,256]{1,0:T(8,128)}, f32[640,256]{1,0:T(8,128)}, f32[256,640]{1,0:T(8,128)}, f32[640,512]{1,0:T(8,128)}, ...) | async-done | bytes 6553616 | tf_op jit(solution)/shard_map/psum | solution.py:220
  (283 shorter events, 185.7 us)
Async XLA Ops:
  7.2 144.0 %copy-start = (f32[512,640]{1,0:T(8,128)S(1)}, f32[512,640]{1,0:T(8,128)}, u32[]{:S(2)}) copy-start(f32[512,640]{1,0:T(8,128)} %param.33) | copy-start | bytes 3932164
  7.2 127.3 %all-reduce.17.cloned.1.call-start = ((), (), s32[]{:S(2)}) async-start(), calls=%async_computation | async-start | bytes 5242880 | tf_op jit(solution)/shard_map/psum | solution.py:146
  71.7 64.9 %copy-start.58 = (f32[640]{0:T(1024)S(1)}, f32[640]{0:T(1024)}, u32[]{:S(2)}) copy-start(f32[640]{0:T(1024)} %param.29) | copy-start | bytes 7684
  71.7 147.3 %all-reduce.19.cloned.1.call-start = ((), (), s32[]{:S(2)}) async-start(), calls=%async_computation.1 | async-start | bytes 5242880 | tf_op jit(solution)/shard_map/psum | solution.py:151
  144.7 101.8 %copy-start.27 = (f32[1024,512]{1,0:T(8,128)}, f32[1024,512]{1,0:T(8,128)S(1)}, u32[]{:S(2)}) copy-start(f32[1024,512]{1,0:T(8,128)S(1)} %fusion.70) | copy-start | bytes 6291460
  158.9 62.3 %copy-start.62 = (f32[640]{0:T(1024)S(1)}, f32[640]{0:T(1024)}, u32[]{:S(2)}) copy-start(f32[640]{0:T(1024)} %param.34) | copy-start | bytes 7684
  158.9 147.7 %all-reduce.21.cloned.1.call-start = ((), (), s32[]{:S(2)}) async-start(), calls=%async_computation.2 | async-start | bytes 5242880 | tf_op jit(solution)/shard_map/psum | solution.py:157
  246.5 277.1 %all-reduce.25.cloned.1.call-start = ((), (), s32[]{:S(2)}) async-start(), calls=%async_computation.4 | async-start | bytes 7864320 | tf_op jit(solution)/shard_map/psum | solution.py:208
  325.9 6.1 copy-start.15
  347.6 10.9 %copy-start.8 = (f32[1,512,1024]{1,2,0:T(8,128)S(1)}, f32[1,512,1024]{1,2,0:T(8,128)}, u32[]{:S(2)}) copy-start(f32[1,512,1024]{1,2,0:T(8,128)} %copy-done.7) | copy-start | bytes 6291460 | tf_op jit(solution)/shard_map/while
  365.5 6.1 copy-start.15
  387.2 10.9 %copy-start.8 = (f32[1,512,1024]{1,2,0:T(8,128)S(1)}, f32[1,512,1024]{1,2,0:T(8,128)}, u32[]{:S(2)}) copy-start(f32[1,512,1024]{1,2,0:T(8,128)} %copy-done.7) | copy-start | bytes 6291460 | tf_op jit(solution)/shard_map/while
  412.1 6.7 copy-start.16
  412.1 6.7 copy-start.49
  431.6 8.0 %copy-start.32 = (f32[1024,1,128]{0,2,1:T(8,128)}, f32[1024,1,128]{0,2,1:T(8,128)S(1)}, u32[]{:S(2)}) copy-start(f32[1024,1,128]{0,2,1:T(8,128)S(1)} %get-tuple-element.300) | copy-start | bytes 1572868
  431.6 8.0 %copy-start.34 = (f32[1024,1,128]{0,2,1:T(8,128)}, f32[1024,1,128]{0,2,1:T(8,128)S(1)}, u32[]{:S(2)}) copy-start(f32[1024,1,128]{0,2,1:T(8,128)S(1)} %get-tuple-element.301) | copy-start | bytes 1572868
  441.8 313.5 %all-reduce.23.cloned.1.call-start = ((), (), s32[]{:S(2)}) async-start(), calls=%async_computation.3 | async-start | bytes 13107200 | tf_op jit(solution)/shard_map/psum | solution.py:220
  443.3 8.8 %copy-start.12 = (f32[1024,640]{1,0:T(8,128)S(1)}, f32[1024,640]{1,0:T(8,128)}, u32[]{:S(2)}) copy-start(f32[1024,640]{1,0:T(8,128)} %copy-done.9) | copy-start | bytes 7864324
  443.3 8.8 %copy-start.38 = (f32[1024,512]{1,0:T(8,128)S(1)}, f32[1024,512]{1,0:T(8,128)}, u32[]{:S(2)}) copy-start(f32[1024,512]{1,0:T(8,128)} %copy-done.36) | copy-start | bytes 6291460
  443.3 8.8 %copy-start.40 = (f32[1024,512]{1,0:T(8,128)S(1)}, f32[1024,512]{1,0:T(8,128)}, u32[]{:S(2)}) copy-start(f32[1024,512]{1,0:T(8,128)} %copy-done.39) | copy-start | bytes 6291460
  452.1 7.3 copy-start.6
  452.1 7.3 copy-start.33
  452.1 7.3 copy-start.35
  452.1 12.9 %copy-start.31 = (f32[32,8,2,512]{3,1,2,0:T(8,128)S(1)}, f32[32,8,2,512]{3,1,2,0:T(8,128)}, u32[]{:S(2)}) copy-start(f32[32,8,2,512]{3,1,2,0:T(8,128)} %copy-done.29) | copy-start | bytes 3145732
  (50 other events, 186.7 us)
Sparse Core Ops, SparseCore 0:
  71.8 62.5 all-reduce.16
  159.0 59.9 all-reduce.18
  246.6 59.9 all-reduce.20
  441.9 81.6 all-reduce.24
  530.1 225.1 all-reduce.22
